TPU v7x, 128 devices: a whole 4x4x4 slice. The times are simulated.
128 devices in a mesh: col: 16 (over y_lo, z, core), row: 8 (over y_hi, x).
Axes of the slice: x: 4, y: 4 (y_hi: 2, y_lo: 2; y = y_hi * 2 + y_lo), z: 4, core: 2. Of those that a mesh axis runs over, the one named last changes fastest.
Arguments:
- matrix: float32 [8192, 8192], P('row', 'col'), may hold values from -64 to 64, as said below
- plan: int32 [3, 16], replicated, may hold values from 0 to 1
Outputs:
- rotated: float32 [8192, 8192], P('row', 'col')
- coupling: float32 [3], replicated
Inputs may be any that keep to these rules, and one draw needn't show every extreme that they name: Entries of the matrix are real numbers; column scales differ between columns.
All inputs are finite; a program needn't handle non-finite values.
Results may differ from a plain program's by a relative error of at most 0.0003.
Values sent between devices are 32-bit elements; how exact they have to be, the bound alone decides.
No kernel may reach another device: no remote copies, remote signals or barrier semaphores. Data moves between devices by JAX's collectives and lax.ppermute only.
A program may use at most 128 MiB of HBM per device.

v0:
```python
import jax
import jax.numpy as jnp
from jax import lax
from jax.sharding import PartitionSpec as P

SWEEPS = 2
STEPS = 3


highest = lax.Precision.HIGHEST
eps = 1e-06


def from_behind(x, axis, by):
    count = lax.axis_size(axis)
    return lax.ppermute(x, axis, [(i, (i + by) % count) for i in range(count)])


def product(first, second):
    return jnp.dot(first, second, precision=highest, preferred_element_type=jnp.float32)


def sweep_rotation(gram):
    width = gram.shape[0]
    eye = jnp.eye(width, dtype=jnp.float32)
    upper = jnp.triu(jnp.ones((width, width), jnp.float32), 1)
    rotation = eye
    for sweep in range(SWEEPS):
        diag = jnp.diagonal(gram)
        ratio = gram / (diag[:, None] + diag[None, :] + eps) * upper
        skew_raw = ratio - ratio.T
        scale = jnp.maximum(jnp.sqrt(jnp.sum(skew_raw * skew_raw)), 1.0)
        skew = skew_raw / scale
        square = product(skew, skew)
        system = eye - square
        inverse = 4.0 / 3.0 * eye - 4.0 / 9.0 * system
        for turn in range(2):
            inverse = product(inverse, 2.0 * eye - product(system, inverse))
        qmat = product(eye - 2.0 * skew + square, inverse)
        gram = product(qmat.T, product(gram, qmat))
        if sweep == 0:
            rotation = qmat
        else:
            rotation = product(rotation, qmat)
    return (rotation, gram)


def local_product(first, second):
    return lax.dot_general(
        first,
        second,
        (((0,), (0,)), ((), ())),
        precision=highest,
        preferred_element_type=jnp.float32,
    )


def pass_on(send):
    return from_behind(send, "col", 1)


def rotate_local(pair, gram, block):
    rotation, turned = sweep_rotation(gram)
    moved = product(pair, rotation)
    cross_sq = jnp.sum(turned[:block, block:] * turned[:block, block:])
    diag_sq = jnp.sum(jnp.diagonal(turned) ** 2)
    return (moved, turned, cross_sq, diag_sq)


def tally_step(cross_sq, diag_sq):
    return lax.psum((cross_sq, diag_sq), "col")


def finish_tally(tallies):
    crosses = jnp.stack([entry[0] for entry in tallies])
    diagonals = jnp.stack([entry[1] for entry in tallies])
    return jnp.log(crosses / diagonals)


def on_device(matrix, plan):
    block = matrix.shape[1] // 2
    position = lax.axis_index("col")
    pair_count = plan.shape[1]
    picker = jnp.arange(pair_count, dtype=jnp.int32) == position
    pair = matrix
    tallies = []
    for step in range(STEPS):
        gram = lax.psum(local_product(pair, pair), "row")
        moved, turned, cross_sq, diag_sq = rotate_local(pair, gram, block)
        tallies.append(tally_step(cross_sq, diag_sq))
        flag = jnp.sum(jnp.where(picker, plan[step], 0)) == 1
        left = moved[:, :block]
        right = moved[:, block:]
        send = jnp.where(flag, right, left)
        keep = jnp.where(flag, left, right)
        received = pass_on(send)
        pair = jnp.concatenate([keep, received], axis=1)
    return (pair, finish_tally(tallies))


def solution(mesh):
    in_specs = (P("row", "col"), P())
    out_specs = (P("row", "col"), P())
    return jax.shard_map(
        on_device, mesh=mesh, in_specs=in_specs, out_specs=out_specs, check_vma=False
    )
```

profile of v0, /device:TPU:1, one launch (start us, length us, event | category | flops | bytes accessed | tf_op | source)
XLA Modules:
  0.0 591.8 jit_solution(386802026403919295)
XLA Ops:
  19.1 80.2 %all-reduce.5.cloned.1.call-done = f32[512,512]{1,0:T(8,128)} async-done(((f32[512,512]{1,0:T(8,128)}), f32[512,512]{1,0:T(8,128)}) %all-reduce.5.cloned.1.call-update) | async-done | bytes 1048592 | tf_op jit(solution)/shard_map/psum | solution.py:88
  99.3 8.6 %gather_fusion = f32[512]{0:T(512)S(1)} fusion(f32[512,512]{1,0:T(8,128)} %all-reduce.5.cloned.1.call-done, s32[512]{0:T(512)S(1)} %bitcast.133), kind=kCustom, calls=%fused_computation | custom fusion | bytes 8192 | tf_op jit(solution)/shard_map/jit(diagonal)/cond/branch_0_fun/gather | solution.py:29
  138.2 4.5 gather_fusion.1
  148.4 5.1 fusion.83
  172.5 6.7 %convolution_bitcast_fusion = f32[1024,512]{0,1:T(8,128)S(1)} fusion(f32[512,512]{1,0:T(8,128)S(1)} %fusion.149, f32[1024,512]{1,0:T(8,128)S(1)} %copy-done), kind=kOutput, calls=%fused_computation.48 | convolution fusion | flops 3221225472 | bytes 5242880 | tf_op jit(solution)/shard_map/dot_general | solution.py:20
  179.4 6.8 %collective-permute-start = (f32[1024,256]{0,1:T(8,128)S(1)}, f32[1024,256]{0,1:T(8,128)S(1)}, u32[]{:S(2)}, u32[]{:S(2)}) collective-permute-start(f32[1024,256]{0,1:T(8,128)S(1)} %get-tuple-element.24), channel_id=1, source_target_pairs={{0,8},{8,16},{16,24},{24,32},{32,40},{40,48},{48,56},{56,64},{64,7... | collective-permute-start | bytes 3145736 | tf_op jit(solution)/shard_map/ppermute | solution.py:16
  186.2 11.7 %collective-permute-done = f32[1024,256]{0,1:T(8,128)S(1)} collective-permute-done((f32[1024,256]{0,1:T(8,128)S(1)}, f32[1024,256]{0,1:T(8,128)S(1)}, u32[]{:S(2)}, u32[]{:S(2)}) %collective-permute-start) | collective-permute-done | bytes 1048608 | tf_op jit(solution)/shard_map/ppermute | solution.py:16
  203.2 80.8 %all-reduce.7.cloned.1.call-done = f32[512,512]{0,1:T(8,128)} async-done(((f32[512,512]{0,1:T(8,128)}), f32[512,512]{0,1:T(8,128)}) %all-reduce.7.cloned.1.call-update) | async-done | bytes 1048592 | tf_op jit(solution)/shard_map/psum | solution.py:88
  284.0 9.6 %gather_fusion.2 = f32[512]{0:T(512)S(1)} fusion(f32[512,512]{0,1:T(8,128)} %all-reduce.7.cloned.1.call-done, s32[512]{0:T(512)S(1)} %bitcast.135), kind=kCustom, calls=%fused_computation.2 | custom fusion | bytes 8192 | tf_op jit(solution)/shard_map/jit(diagonal)/cond/branch_0_fun/gather | solution.py:29
  298.2 5.7 fusion.140
  321.7 4.5 gather_fusion.3
  331.8 5.0 fusion.84
  361.2 6.9 %collective-permute-start.1 = (f32[1024,256]{0,1:T(8,128)}, f32[1024,256]{0,1:T(8,128)}, u32[]{:S(2)}, u32[]{:S(2)}) collective-permute-start(f32[1024,256]{0,1:T(8,128)} %get-tuple-element.22), channel_id=1, source_target_pairs={{0,8},{8,16},{16,24},{24,32},{32,40},{40,48},{48,56},{56,64},{64,7... | collective-permute-start | bytes 3145736 | tf_op jit(solution)/shard_map/ppermute | solution.py:16
  371.6 8.6 %collective-permute-done.1 = f32[1024,256]{0,1:T(8,128)} collective-permute-done((f32[1024,256]{0,1:T(8,128)}, f32[1024,256]{0,1:T(8,128)}, u32[]{:S(2)}, u32[]{:S(2)}) %collective-permute-start.1) | collective-permute-done | bytes 1048608 | tf_op jit(solution)/shard_map/ppermute | solution.py:16
  380.1 6.1 %fusion.1 = f32[512,512]{0,1:T(8,128)} fusion(f32[1024,256]{0,1:T(8,128)} %collective-permute-done.1, f32[1024,256]{0,1:T(8,128)S(1)} %copy-done.24), kind=kOutput, calls=%fused_computation.40 | convolution fusion | flops 3221749760 | bytes 3145728 | tf_op jit(solution)/shard_map/dot_general | solution.py:49
  389.3 4.5 gather_fusion.6
  399.0 4.5 gather_fusion.7
  404.2 63.6 %all-reduce.9.cloned.1.call-done = f32[512,512]{0,1:T(8,128)} async-done(((f32[512,512]{0,1:T(8,128)}), f32[512,512]{0,1:T(8,128)}) %all-reduce.9.cloned.1.call-update) | async-done | bytes 1048592 | tf_op jit(solution)/shard_map/psum | solution.py:88
  467.8 8.8 %gather_fusion.4 = f32[512]{0:T(512)S(1)} fusion(f32[512,512]{0,1:T(8,128)} %all-reduce.9.cloned.1.call-done, s32[512]{0:T(512)S(1)} %bitcast.139), kind=kCustom, calls=%fused_computation.4 | custom fusion | bytes 8192 | tf_op jit(solution)/shard_map/jit(diagonal)/cond/branch_0_fun/gather | solution.py:29
  494.8 4.5 gather_fusion.5
  526.0 4.8 fusion
  531.9 6.7 %collective-permute-start.2 = (f32[1024,256]{0,1:T(8,128)}, f32[1024,256]{0,1:T(8,128)}, u32[]{:S(2)}, u32[]{:S(2)}) collective-permute-start(f32[1024,256]{0,1:T(8,128)} %get-tuple-element.20), channel_id=1, source_target_pairs={{0,8},{8,16},{16,24},{24,32},{32,40},{40,48},{48,56},{56,64},{64,7... | collective-permute-start | bytes 3145736 | tf_op jit(solution)/shard_map/ppermute | solution.py:16
  543.0 4.5 gather_fusion.8
  548.9 26.1 %all-reduce = (f32[1]{0:T(128)}, f32[1]{0:T(128)}, f32[1]{0:T(128)}, f32[1]{0:T(128)}, f32[1]{0:T(128)}, /*index=5*/f32[1]{0:T(128)}) all-reduce(f32[1]{0:T(128)} %bitcast.16, f32[1]{0:T(128)} %bitcast.15, f32[1]{0:T(128)} %bitcast.14, f32[1]{0:T(128)} %bitcast.13, f32[1]{0:T(128)} %bitcast.12, ...), channel_id=1, replica_groups=mesh['col'=16,'row'=8] {'col'}, use_global_device_ids=true, to_apply=%region_23.24 | all-reduce | flops 6 | bytes 48 | tf_op jit(solution)/shard_map/psum | solution.py:71
  (183 shorter events, 191.8 us)
Async XLA Ops:
  7.2 92.1 %all-reduce.5.cloned.1.call-start = ((), (), s32[]{:S(2)}) async-start(), calls=%async_computation | async-start | bytes 2097152 | tf_op jit(solution)/shard_map/psum | solution.py:88
  13.3 270.8 %all-reduce.7.cloned.1.call-start = ((), (), s32[]{:S(2)}) async-start(), calls=%async_computation.1 | async-start | bytes 2097152 | tf_op jit(solution)/shard_map/psum | solution.py:88
  14.9 2.7 copy-start.40
  107.9 3.7 copy-start.8
  160.0 3.6 copy-start.15
  167.4 3.2 copy-start.13
  179.4 23.0 %copy-start.26 = (f32[1024,256]{0,1:T(8,128)}, f32[1024,256]{0,1:T(8,128)S(1)}, u32[]{:S(2)}) copy-start(f32[1024,256]{0,1:T(8,128)S(1)} %get-tuple-element.23) | copy-start | bytes 3145732
  179.4 18.5 %collective-permute-start = (f32[1024,256]{0,1:T(8,128)S(1)}, f32[1024,256]{0,1:T(8,128)S(1)}, u32[]{:S(2)}, u32[]{:S(2)}) collective-permute-start(f32[1024,256]{0,1:T(8,128)S(1)} %get-tuple-element.24), channel_id=1, source_target_pairs={{0,8},{8,16},{16,24},{24,32},{32,40},{40,48},{48,56},{56,64},{64,7... | collective-permute-start | bytes 3145736 | tf_op jit(solution)/shard_map/ppermute | solution.py:16
  198.0 4.5 copy-start.38
  202.5 265.3 %all-reduce.9.cloned.1.call-start = ((), (), s32[]{:S(2)}) async-start(), calls=%async_computation.2 | async-start | bytes 2097152 | tf_op jit(solution)/shard_map/psum | solution.py:88
  284.0 9.6 %copy-start.3 = (f32[512,512]{0,1:T(8,128)S(1)}, f32[512,512]{0,1:T(8,128)}, u32[]{:S(2)}) copy-start(f32[512,512]{0,1:T(8,128)} %all-reduce.7.cloned.1.call-done) | copy-start | bytes 3145732
  293.9 3.6 copy-start.20
  303.9 3.0 copy-start.16
  308.3 3.6 copy-start.17
  311.9 3.8 copy-start.28
  343.4 3.6 copy-start.19
  359.7 9.0 %copy-start.5 = (f32[512,512]{1,0:T(8,128)S(1)}, f32[512,512]{1,0:T(8,128)}, u32[]{:S(2)}) copy-start(f32[512,512]{1,0:T(8,128)} %copy-done.4) | copy-start | bytes 3145732
  361.2 18.9 %collective-permute-start.1 = (f32[1024,256]{0,1:T(8,128)}, f32[1024,256]{0,1:T(8,128)}, u32[]{:S(2)}, u32[]{:S(2)}) collective-permute-start(f32[1024,256]{0,1:T(8,128)} %get-tuple-element.22), channel_id=1, source_target_pairs={{0,8},{8,16},{16,24},{24,32},{32,40},{40,48},{48,56},{56,64},{64,7... | collective-permute-start | bytes 3145736 | tf_op jit(solution)/shard_map/ppermute | solution.py:16
  368.7 11.4 %copy-start.24 = (f32[1024,256]{0,1:T(8,128)S(1)}, f32[1024,256]{0,1:T(8,128)}, u32[]{:S(2)}) copy-start(f32[1024,256]{0,1:T(8,128)} %get-tuple-element.21) | copy-start | bytes 3145732
  389.3 5.9 copy-start.7
  467.8 8.8 %copy-start.2 = (f32[512,512]{0,1:T(8,128)S(1)}, f32[512,512]{0,1:T(8,128)}, u32[]{:S(2)}) copy-start(f32[512,512]{0,1:T(8,128)} %all-reduce.9.cloned.1.call-done) | copy-start | bytes 3145732
  507.1 3.2 copy-start.29
  531.9 47.2 %collective-permute-start.2 = (f32[1024,256]{0,1:T(8,128)}, f32[1024,256]{0,1:T(8,128)}, u32[]{:S(2)}, u32[]{:S(2)}) collective-permute-start(f32[1024,256]{0,1:T(8,128)} %get-tuple-element.20), channel_id=1, source_target_pairs={{0,8},{8,16},{16,24},{24,32},{32,40},{40,48},{48,56},{56,64},{64,7... | collective-permute-start | bytes 3145736 | tf_op jit(solution)/shard_map/ppermute | solution.py:16
  579.1 6.0 %copy-start.1 = (f32[1024,512]{1,0:T(8,128)S(1)}, f32[1024,512]{1,0:T(8,128)}, u32[]{:S(2)}) copy-start(f32[1024,512]{1,0:T(8,128)} %param.2) | copy-start | bytes 6291460
  (23 other events, 39.9 us)
Sparse Core Ops, SparseCore 0:
  13.4 85.8 all-reduce.4
  202.6 81.4 all-reduce.6
  386.4 81.3 all-reduce.8
where the time goes:
time: 601 us; the launch traced here: 592 us
  waiting for transfers between devices  245 us (41%)
  matrix products  154 us (26%)
  local copies, waits for them, and re-layouts  87.7 us (15%)
  other arithmetic  37.7 us (6%)
  blocking collectives  26.1 us (4%)
  between operations  21.1 us (4%)
  starting transfers between devices  20.5 us (3%)
    psum x3, waiting for transfers between devices, on_device(): gram = lax.psum(local_product(pair, pair), 'row')  225 us
    dot_general x54, matrix products, product(): jnp.dot(first, second, precision=highest, preferred_element_type=jnp.floa...  139 us
    gather x6, local copies, waits for them, and re-layouts, sweep_rotation(): diag = jnp.diagonal(gram)  40.6 us
    psum x1, blocking collectives, tally_step(): return lax.psum((cross_sq, diag_sq), 'col')  26.1 us
    ppermute x3, starting transfers between devices, from_behind(): return lax.ppermute(x, axis, [(i, (i + by) % count) for i in range(count)])  20.4 us
    ppermute x3, waiting for transfers between devices, from_behind(): return lax.ppermute(x, axis, [(i, (i + by) % count) for i in range(count)])  20.3 us
    reduce_sum x6, other arithmetic, sweep_rotation(): scale = jnp.maximum(jnp.sqrt(jnp.sum(skew_raw * skew_raw)), 1.0)  15.4 us
    dot_general x3, matrix products, local_product(): lax.dot_general(first, second, (((0,), (0,)), ((), ())), precision=highes...  15.1 us
  transfers between devices with their start and end apart: 6, of which 5 were waited for; matrix products, arithmetic and copies ran while one was open for 7% of the time, Pallas kernels for 0%

commit v1 on v0

v1 whole, which is shorter than its diff:
```python
import functools

import jax
import jax.numpy as jnp
from jax import lax
from jax.experimental import pallas as pl
from jax.experimental.pallas import tpu as pltpu
from jax.sharding import PartitionSpec as P

SWEEPS = 2
STEPS = 3
TILE = 128
VMEM_LIMIT = 56 * 2**20

f32 = jnp.float32
bf16 = jnp.bfloat16
eps = 1e-06
in_vmem = pl.BlockSpec(memory_space=pltpu.VMEM)
in_smem = pl.BlockSpec(memory_space=pltpu.SMEM)


def split(x):
    high = x.astype(bf16)
    return high, (x - high.astype(f32)).astype(bf16)


def dot(first, second):
    return jnp.dot(first, second, preferred_element_type=f32)


def dot_t(first, second):
    return lax.dot_general(first, second, (((0,), (0,)), ((), ())), preferred_element_type=f32)


def triple(op, first, second):
    return op(first[0], second[0]) + (op(first[0], second[1]) + op(first[1], second[0]))


mul = functools.partial(triple, dot)
mul_t = functools.partial(triple, dot_t)


def columns(parts, start, size):
    return tuple(part[:, start : start + size] for part in parts)


def call(body, outs, in_specs, flops, name, **kwargs):
    return pl.pallas_call(
        body,
        out_shape=outs,
        in_specs=in_specs,
        out_specs=jax.tree.map(lambda _: in_vmem, outs),
        compiler_params=pltpu.CompilerParams(vmem_limit_bytes=VMEM_LIMIT),
        cost_estimate=pl.CostEstimate(flops=flops, bytes_accessed=4 * 2**20, transcendentals=0),
        name=name,
        **kwargs,
    )


def shape(*dims):
    return jax.ShapeDtypeStruct(dims, f32)


def tile_pairs(width):
    count = width // TILE
    return [(i, j) for i in range(count) for j in range(i, count)]


def gram_body(pair_ref, out_ref):
    parts = split(pair_ref[...])
    width = pair_ref.shape[1]
    half = width // 2
    blocks = {}
    for i, j in ((0, 0), (0, 1), (1, 1)):
        blocks[i, j] = mul_t(columns(parts, i * half, half), columns(parts, j * half, half))
    per = half // TILE
    for at, (i, j) in enumerate(tile_pairs(width)):
        block = blocks[i // per, j // per]
        r, c = (i % per) * TILE, (j % per) * TILE
        out_ref[at * TILE : (at + 1) * TILE, :] = block[r : r + TILE, c : c + TILE]


def local_gram(pair):
    rows, width = pair.shape
    count = len(tile_pairs(width))
    return call(gram_body, shape(count * TILE, TILE), [in_vmem], 6 * rows * width * width, "local_gram")(pair)


def cross_body(first_ref, second_ref, out_ref):
    out_ref[...] = mul_t(split(first_ref[...]), split(second_ref[...]))


def local_cross(first, second):
    rows, block = first.shape
    return call(cross_body, shape(block, block), [in_vmem] * 2, 6 * rows * block * block, "local_cross")(first, second)


def sweep(gram, row, col):
    eye = row == col
    one = eye.astype(f32)
    on_diag = jnp.where(eye, gram, 0.0)
    diag_sum = jnp.sum(on_diag, axis=0, keepdims=True) + jnp.sum(on_diag, axis=1, keepdims=True)
    ratio = gram / (diag_sum + eps)
    skew = jnp.where(col > row, ratio, jnp.where(row > col, -ratio, 0.0))
    norm = jnp.sum(jnp.sum(skew * skew, axis=0, keepdims=True), axis=1, keepdims=True)
    skew = skew * (1.0 / jnp.maximum(jnp.sqrt(norm), 1.0))
    skew_parts = split(skew)
    square = mul(skew_parts, skew_parts)
    t1 = one * (1.0 / 3.0) + square * (2.0 / 3.0)
    t1_parts = split(t1)
    t2 = mul(t1_parts, t1_parts)
    t2_parts = split(t2)
    t4 = mul(t2_parts, t2_parts)
    low = one + t1 + t2 + mul(t1_parts, t2_parts)
    inverse = (low + mul(split(low), split(t4))) * (2.0 / 3.0)
    qmat = mul(split(one - 2.0 * skew + square), split(inverse))
    q_parts = split(qmat)
    return qmat, q_parts, mul(split(gram), q_parts)


def rotate(gram, pair_left, pair_right, flag, outs):
    send_ref, keep_rot_ref, send_diag_ref, keep_diag_ref, stat_ref = outs
    width = gram.shape[0]
    half = width // 2
    row = lax.broadcasted_iota(jnp.int32, (width, width), 0)
    col = lax.broadcasted_iota(jnp.int32, (width, width), 1)
    _, first, half_turned = sweep(gram, row, col)
    gram = mul_t(first, split(half_turned))
    _, second, half_turned = sweep(gram, row, col)
    rotation = mul(first, second)
    turned = split(half_turned)
    left, right = columns(second, 0, half), columns(second, half, half)
    left_diag = mul_t(left, columns(turned, 0, half))
    right_diag = mul_t(right, columns(turned, half, half))
    cross = mul_t(left, columns(turned, half, half))
    cross_sq = jnp.sum(jnp.sum(cross * cross, axis=0, keepdims=True), axis=1, keepdims=True)
    eye = row[:half, :half] == col[:half, :half]
    on_diag = jnp.where(eye, left_diag * left_diag + right_diag * right_diag, 0.0)
    diag_sq = jnp.sum(jnp.sum(on_diag, axis=0, keepdims=True), axis=1, keepdims=True)
    lane = lax.broadcasted_iota(jnp.int32, stat_ref.shape, 1)
    stat_ref[...] = jnp.where(lane == 0, cross_sq, jnp.where(lane == 1, diag_sq, 0.0))
    send_rot = jnp.where(flag, rotation[:, half:], rotation[:, :half])
    keep_rot_ref[...] = jnp.where(flag, rotation[:, :half], rotation[:, half:])
    send_diag_ref[...] = jnp.where(flag, right_diag, left_diag)
    keep_diag_ref[...] = jnp.where(flag, left_diag, right_diag)
    rot = split(send_rot)
    top, bottom = tuple(p[:half] for p in rot), tuple(p[half:] for p in rot)
    send_ref[...] = mul(split(pair_left), top) + mul(split(pair_right), bottom)


def first_body(flag_ref, tiles_ref, pair_ref, *refs):
    outs, gram_ref = refs[:-1], refs[-1]
    width = pair_ref.shape[1]
    half = width // 2
    for at, (i, j) in enumerate(tile_pairs(width)):
        tile = tiles_ref[at * TILE : (at + 1) * TILE, :]
        gram_ref[i * TILE : (i + 1) * TILE, j * TILE : (j + 1) * TILE] = tile
        if i != j:
            gram_ref[j * TILE : (j + 1) * TILE, i * TILE : (i + 1) * TILE] = tile.T
    flag = flag_ref[0] == 1
    rotate(gram_ref[...], pair_ref[:, :half], pair_ref[:, half:], flag, outs)


def later_body(flag_ref, left_diag_ref, cross_ref, right_diag_ref, left_ref, right_ref, *refs):
    outs, gram_ref = refs[:-1], refs[-1]
    half = cross_ref.shape[0]
    cross = cross_ref[...]
    gram_ref[:half, :half] = left_diag_ref[...]
    gram_ref[:half, half:] = cross
    gram_ref[half:, :half] = cross.T
    gram_ref[half:, half:] = right_diag_ref[...]
    flag = flag_ref[0] == 1
    rotate(gram_ref[...], left_ref[...], right_ref[...], flag, outs)


def rotation_call(body, operands, rows, half, name):
    width = 2 * half
    outs = [
        shape(rows, half),
        shape(width, half),
        shape(half, half),
        shape(half, half),
        shape(1, TILE),
    ]
    specs = [in_smem] + [in_vmem] * (len(operands) - 1)
    scratch = [pltpu.VMEM((width, width), f32)]
    return call(body, outs, specs, 102 * width**3, name, scratch_shapes=scratch)(*operands)


def keep_body(left_ref, right_ref, rot_ref, out_ref):
    rot = split(rot_ref[...])
    half = rot_ref.shape[1]
    top, bottom = tuple(p[:half] for p in rot), tuple(p[half:] for p in rot)
    out_ref[...] = mul(split(left_ref[...]), top) + mul(split(right_ref[...]), bottom)


def kept(left, right, rot):
    rows, half = left.shape
    return call(keep_body, shape(rows, half), [in_vmem] * 3, 12 * rows * half * half, "kept")(left, right, rot)


def join_body(left_ref, right_ref, out_ref):
    half = left_ref.shape[1]
    out_ref[:, :half] = left_ref[...]
    out_ref[:, half:] = right_ref[...]


def from_behind(x):
    count = lax.axis_size("col")
    return lax.ppermute(x, "col", [(i, (i + 1) % count) for i in range(count)])


def sum_over_rows(x):
    count = lax.axis_size("row")
    slices = x.reshape(count, x.shape[0] // count, x.shape[1])
    mine = jnp.sum(lax.all_to_all(slices, "row", 0, 0), axis=0)
    shared = jnp.broadcast_to(mine[None], slices.shape)
    return lax.all_to_all(shared, "row", 0, 0).reshape(x.shape)


def sum_over_pairs(x):
    count = lax.axis_size("col")
    shared = jnp.broadcast_to(x, (count, x.shape[1]))
    return jnp.sum(lax.all_to_all(shared, "col", 0, 0, tiled=True), axis=0)


def on_device(matrix, plan):
    rows, width = matrix.shape
    half = width // 2
    position = lax.axis_index("col")
    flags = lax.dynamic_slice_in_dim(plan, position, 1, axis=1)
    left, right = matrix[:, :half], matrix[:, half:]
    stats = []
    for step in range(STEPS):
        if step == 0:
            gram = sum_over_rows(local_gram(matrix))
            made = rotation_call(first_body, (flags[0], gram, matrix), rows, half, "rotate_first")
        else:
            cross = sum_over_rows(local_cross(left, right))
            operands = (flags[step], left_diag, cross, right_diag, left, right)
            made = rotation_call(later_body, operands, rows, half, "rotate_later")
        send, keep_rot, send_diag, left_diag, stat = made
        stats.append(stat)
        received = from_behind(send)
        if step < STEPS - 1:
            right_diag = from_behind(send_diag)
        left = kept(left, right, keep_rot)
        right = received
    sums = sum_over_pairs(jnp.concatenate(stats, axis=1)).reshape(STEPS, TILE)
    rotated = call(join_body, shape(rows, width), [in_vmem] * 2, 0, "join")(left, right)
    return rotated, jnp.log(sums[:, 0] / sums[:, 1])


def solution(mesh):
    in_specs = (P("row", "col"), P())
    out_specs = (P("row", "col"), P())
    return jax.shard_map(
        on_device, mesh=mesh, in_specs=in_specs, out_specs=out_specs, check_vma=False
    )
```

time: 601 us -> 235 us (0.39)
  waiting for transfers between devices: 245 us -> 59.4 us
  matrix products: 154 us -> 0 us
  Pallas kernels: 0 us -> 96.6 us
  local copies, waits for them, and re-layouts: 87.7 us -> 10.3 us
  other arithmetic: 37.7 us -> 1.5 us
  starting transfers between devices: 20.5 us -> 41.6 us
  between operations: 21.1 us -> 0.96 us
  blocking collectives: 26.1 us -> 19.8 us
    psum x3 -> x0, waiting for transfers between devices: 225 us -> none  [on_device(): gram = lax.psum(local_product(pair, pair), 'row')]
    dot_general x57 -> x0, matrix products: 154 us -> none  [the longest x54 139 us: product(): jnp.dot(first, second, precision=highest, preferred_element_type=jnp.floa...]
    pallas_call x0 -> x10, Pallas kernels: none -> 96.6 us  [the longest x3 73 us: rotation_call(): call(body, outs, specs, 102 * width ** 3, name, scratch_shapes=scratch)]
    gather x9 -> x0, local copies, waits for them, and re-layouts: 54.1 us -> none  [the longest x6 40.6 us: sweep_rotation(): diag = jnp.diagonal(gram)]
    all_to_all x0 -> x6, waiting for transfers between devices: none -> 44 us  [the longest x3 27.5 us: sum_over_rows(): return lax.all_to_all(shared, 'row', 0, 0).reshape(x.shape)]
    psum x1 -> x0, blocking collectives: 26.1 us -> none  [tally_step(): return lax.psum((cross_sq, diag_sq), 'col')]
    all_to_all x0 -> x6, starting transfers between devices: none -> 24.9 us  [the longest x3 10.4 us: sum_over_rows(): return lax.all_to_all(shared, 'row', 0, 0).reshape(x.shape)]
    reduce_sum x13 -> x4, other arithmetic: 20.2 us -> 0.11 us  [the longest x3 0.07 us: sum_over_rows(): mine = jnp.sum(lax.all_to_all(slices, 'row', 0, 0), axis=0)]
  transfers between devices with their start and end apart: 6 -> 11, of which waited for: 5 -> 8; matrix products, arithmetic and copies ran while one was open for 7% -> 2% of each run, Pallas kernels for 0% -> 5%
where the time goes in v1:
time: 235 us; the launch traced here: 230 us
  Pallas kernels  96.6 us (41%)
  waiting for transfers between devices  59.4 us (25%)
  starting transfers between devices  41.6 us (18%)
  blocking collectives  19.8 us (8%)
  local copies, waits for them, and re-layouts  10.3 us (4%)
    pallas_call x3, Pallas kernels, rotation_call(): call(body, outs, specs, 102 * width ** 3, name, scratch_shapes=scratch)  73 us
    all_to_all x3, waiting for transfers between devices, sum_over_rows(): return lax.all_to_all(shared, 'row', 0, 0).reshape(x.shape)  27.5 us
    all_to_all x1, blocking collectives, sum_over_rows(): mine = jnp.sum(lax.all_to_all(slices, 'row', 0, 0), axis=0)  19.8 us
    ppermute x5, starting transfers between devices, from_behind(): return lax.ppermute(x, 'col', [(i, (i + 1) % count) for i in range(count)])  16.7 us
    ppermute x5, waiting for transfers between devices, from_behind(): return lax.ppermute(x, 'col', [(i, (i + 1) % count) for i in range(count)])  15.4 us
    pallas_call x3, Pallas kernels, kept(): call(keep_body, shape(rows, half), [in_vmem] * 3, 12 * rows * half * half...  10.9 us
    all_to_all x3, starting transfers between devices, sum_over_rows(): return lax.all_to_all(shared, 'row', 0, 0).reshape(x.shape)  10.4 us
    all_to_all x2, waiting for transfers between devices, sum_over_rows(): mine = jnp.sum(lax.all_to_all(slices, 'row', 0, 0), axis=0)  10.2 us
  transfers between devices with their start and end apart: 11, of which 8 were waited for; matrix products, arithmetic and copies ran while one was open for 2% of the time, Pallas kernels for 5%

profile of v1, /device:TPU:1, one launch (start us, length us, event | category | flops | bytes accessed | tf_op | source)
XLA Modules:
  0.0 230.2 jit_solution(14384211815522901025)
XLA Ops:
  0.6 3.9 %local_gram.1 = f32[1280,128]{1,0:T(8,128)} custom-call(f32[1024,512]{1,0:T(8,128)} %pair_ref.3), custom_call_target="tpu_custom_call" | custom-call | flops 1610612736 | bytes 4194304 | tf_op jit(solution)/shard_map/local_gram/pallas_call | solution.py:86
  4.5 19.8 %all_to_all.36 = f32[8,160,128]{2,1,0:T(8,128)S(1)} all-to-all(f32[8,160,128]{2,1,0:T(8,128)} %bitcast.13), channel_id=1, replica_groups=mesh['col'=16,'row'=8] {'row'}, dimensions={0} | all-to-all | bytes 1310720 | tf_op jit(solution)/shard_map/all_to_all | solution.py:216
  25.3 3.5 %all-to-all-start.1 = ((f32[8,160,128]{2,1,0:T(8,128)}), f32[8,160,128]{2,1,0:T(8,128)S(1)}, u32[]{:S(2)}, u32[]{:S(2)}) async-start(f32[8,160,128]{2,1,0:T(8,128)} %broadcast_in_dim.8), calls=%async_computation.1 | async-start | bytes 1310720 | tf_op jit(solution)/shard_map/all_to_all | solution.py:218
  29.5 12.3 %all-to-all-done.1 = f32[8,160,128]{2,1,0:T(8,128)S(1)} async-done(((f32[8,160,128]{2,1,0:T(8,128)}), f32[8,160,128]{2,1,0:T(8,128)S(1)}, u32[]{:S(2)}, u32[]{:S(2)}) %all-to-all-start.1) | async-done | bytes 655392 | tf_op jit(solution)/shard_map/all_to_all | solution.py:218
  42.7 20.6 %rotate_first.1 = (f32[1024,256]{1,0:T(8,128)}, f32[512,256]{1,0:T(8,128)}, f32[256,256]{1,0:T(8,128)}, f32[256,256]{1,0:T(8,128)}, f32[1,128]{1,0:T(1,128)}) custom-call(s32[1]{0:T(128)} %bitcast.flag_ref, f32[1280,128]{1,0:T(8,128)} %bitcast.12, f32[1024,512]{1,0:T(8,128)} %pair_ref.3), custom_call_target="tpu_custom_call" | custom-call | flops 13690208256 | bytes 4194304 | tf_op jit(solution)/shard_map/rotate_first/pallas_call | solution.py:187
  67.2 3.6 %kept.3.first_ref.left_ref = f32[1024,256]{1,0:T(8,128)} custom-call(f32[1024,256]{1,0:T(8,128)} %get-tuple-element.29.left_ref, f32[1024,256]{1,0:T(8,128)} %get-tuple-element.28.right_ref, f32[512,256]{1,0:T(8,128)} %get-tuple-element.15.rot_ref), custom_call_target="tpu_custom_call" | custom-call | flops 805306368 | bytes 4194304 | tf_op jit(solution)/shard_map/kept/pallas_call | solution.py:199
  70.8 7.0 %collective-permute-done.second_ref.right_ref = f32[1024,256]{1,0:T(8,128)S(1)} collective-permute-done((f32[1024,256]{1,0:T(8,128)}, f32[1024,256]{1,0:T(8,128)S(1)}, u32[]{:S(2)}, u32[]{:S(2)}) %collective-permute-start) | collective-permute-done | bytes 1048608 | tf_op jit(solution)/shard_map/ppermute | solution.py:210
  81.6 3.4 %all-to-all-start.2 = ((f32[8,32,256]{2,1,0:T(8,128)}), f32[8,32,256]{2,1,0:T(8,128)S(1)}, u32[]{:S(2)}, u32[]{:S(2)}) async-start(f32[8,32,256]{2,1,0:T(8,128)} %bitcast.10), calls=%async_computation.2 | async-start | bytes 524288 | tf_op jit(solution)/shard_map/all_to_all | solution.py:216
  87.5 5.1 %all-to-all-done.2 = f32[8,32,256]{2,1,0:T(8,128)S(1)} async-done(((f32[8,32,256]{2,1,0:T(8,128)}), f32[8,32,256]{2,1,0:T(8,128)S(1)}, u32[]{:S(2)}, u32[]{:S(2)}) %all-to-all-start.2) | async-done | bytes 262176 | tf_op jit(solution)/shard_map/all_to_all | solution.py:216
  93.3 3.4 %all-to-all-start.3 = ((f32[8,32,256]{2,1,0:T(8,128)}), f32[8,32,256]{2,1,0:T(8,128)S(1)}, u32[]{:S(2)}, u32[]{:S(2)}) async-start(f32[8,32,256]{2,1,0:T(8,128)} %broadcast_in_dim.9), calls=%async_computation.3 | async-start | bytes 524288 | tf_op jit(solution)/shard_map/all_to_all | solution.py:218
  96.8 7.6 %all-to-all-done.3 = f32[8,32,256]{2,1,0:T(8,128)S(1)} async-done(((f32[8,32,256]{2,1,0:T(8,128)}), f32[8,32,256]{2,1,0:T(8,128)S(1)}, u32[]{:S(2)}, u32[]{:S(2)}) %all-to-all-start.3) | async-done | bytes 262176 | tf_op jit(solution)/shard_map/all_to_all | solution.py:218
  105.0 32.3 %rotate_later.2 = (f32[1024,256]{1,0:T(8,128)}, f32[512,256]{1,0:T(8,128)}, f32[256,256]{1,0:T(8,128)}, f32[256,256]{1,0:T(8,128)}, f32[1,128]{1,0:T(1,128)}) custom-call(s32[1]{0:T(128)} %bitcast.3.flag_ref, f32[256,256]{1,0:T(8,128)} %get-tuple-element.17.left_diag_ref, f32[256,256]{1,0:T(8,128)} %bitcast.15, f32[256,256]{1,0:T(8,128)} %copy-done.13, ...), custom_call_target="tpu_custom_call" | custom-call | flops 13690208256 | bytes 4194304 | tf_op jit(solution)/shard_map/rotate_later/pallas_call | solution.py:187
  137.3 4.7 %collective-permute-start.2 = (f32[1024,256]{1,0:T(8,128)}, f32[1024,256]{1,0:T(8,128)S(1)}, u32[]{:S(2)}, u32[]{:S(2)}) collective-permute-start(f32[1024,256]{1,0:T(8,128)} %get-tuple-element.20), channel_id=1, source_target_pairs={{0,8},{8,16},{16,24},{24,32},{32,40},{40,48},{48,56},{56,64},{64,7... | collective-permute-start | bytes 3145736 | tf_op jit(solution)/shard_map/ppermute | solution.py:210
  142.1 3.7 %kept.4.first_ref.left_ref = f32[1024,256]{1,0:T(8,128)} custom-call(f32[1024,256]{1,0:T(8,128)} %kept.3.first_ref.left_ref, f32[1024,256]{1,0:T(8,128)} %copy-done.2, f32[512,256]{1,0:T(8,128)} %get-tuple-element.19.rot_ref), custom_call_target="tpu_custom_call" | custom-call | flops 805306368 | bytes 4194304 | tf_op jit(solution)/shard_map/kept/pallas_call | solution.py:199
  145.7 8.4 %collective-permute-done.2.second_ref.right_ref = f32[1024,256]{1,0:T(8,128)S(1)} collective-permute-done((f32[1024,256]{1,0:T(8,128)}, f32[1024,256]{1,0:T(8,128)S(1)}, u32[]{:S(2)}, u32[]{:S(2)}) %collective-permute-start.2) | collective-permute-done | bytes 1048608 | tf_op jit(solution)/shard_map/ppermute | solution.py:210
  158.0 3.4 %all-to-all-start.4 = ((f32[8,32,256]{2,1,0:T(8,128)}), f32[8,32,256]{2,1,0:T(8,128)S(1)}, u32[]{:S(2)}, u32[]{:S(2)}) async-start(f32[8,32,256]{2,1,0:T(8,128)} %bitcast.11), calls=%async_computation.4 | async-start | bytes 524288 | tf_op jit(solution)/shard_map/all_to_all | solution.py:216
  163.8 5.1 %all-to-all-done.4 = f32[8,32,256]{2,1,0:T(8,128)S(1)} async-done(((f32[8,32,256]{2,1,0:T(8,128)}), f32[8,32,256]{2,1,0:T(8,128)S(1)}, u32[]{:S(2)}, u32[]{:S(2)}) %all-to-all-start.4) | async-done | bytes 262176 | tf_op jit(solution)/shard_map/all_to_all | solution.py:216
  169.7 3.4 %all-to-all-start.5 = ((f32[8,32,256]{2,1,0:T(8,128)}), f32[8,32,256]{2,1,0:T(8,128)S(1)}, u32[]{:S(2)}, u32[]{:S(2)}) async-start(f32[8,32,256]{2,1,0:T(8,128)} %broadcast_in_dim.10), calls=%async_computation.5 | async-start | bytes 524288 | tf_op jit(solution)/shard_map/all_to_all | solution.py:218
  173.1 7.6 %all-to-all-done.5 = f32[8,32,256]{2,1,0:T(8,128)S(1)} async-done(((f32[8,32,256]{2,1,0:T(8,128)}), f32[8,32,256]{2,1,0:T(8,128)S(1)}, u32[]{:S(2)}, u32[]{:S(2)}) %all-to-all-start.5) | async-done | bytes 262176 | tf_op jit(solution)/shard_map/all_to_all | solution.py:218
  181.4 20.1 %rotate_later.3 = (f32[1024,256]{1,0:T(8,128)}, f32[512,256]{1,0:T(8,128)}, f32[256,256]{1,0:T(8,128)}, f32[256,256]{1,0:T(8,128)}, f32[1,128]{1,0:T(1,128)}) custom-call(s32[1]{0:T(128)} %bitcast.6.flag_ref, f32[256,256]{1,0:T(8,128)} %get-tuple-element.21.left_diag_ref, f32[256,256]{1,0:T(8,128)} %bitcast.14, f32[256,256]{1,0:T(8,128)} %copy-done.12, ...), custom_call_target="tpu_custom_call" | custom-call | flops 13690208256 | bytes 4194304 | tf_op jit(solution)/shard_map/rotate_later/pallas_call | solution.py:187
  201.5 4.7 %collective-permute-start.4 = (f32[1024,256]{1,0:T(8,128)}, f32[1024,256]{1,0:T(8,128)S(1)}, u32[]{:S(2)}, u32[]{:S(2)}) collective-permute-start(f32[1024,256]{1,0:T(8,128)} %get-tuple-element.24), channel_id=1, source_target_pairs={{0,8},{8,16},{16,24},{24,32},{32,40},{40,48},{48,56},{56,64},{64,7... | collective-permute-start | bytes 3145736 | tf_op jit(solution)/shard_map/ppermute | solution.py:210
  207.5 7.8 %all-to-all-start.6 = ((f32[16,1,384]{2,1,0:T(1,128)}), f32[16,1,384]{2,1,0:T(1,128)S(1)}, u32[]{:S(2)}, u32[]{:S(2)}) async-start(f32[16,1,384]{2,1,0:T(1,128)} %broadcast_in_dim.11), calls=%async_computation.6 | async-start | bytes 49152 | tf_op jit(solution)/shard_map/all_to_all | solution.py:224
  215.3 3.6 %kept.5.left_ref = f32[1024,256]{1,0:T(8,128)} custom-call(f32[1024,256]{1,0:T(8,128)} %kept.4.first_ref.left_ref, f32[1024,256]{1,0:T(8,128)} %copy-done.1, f32[512,256]{1,0:T(8,128)} %get-tuple-element.23.rot_ref), custom_call_target="tpu_custom_call" | custom-call | flops 805306368 | bytes 4194304 | tf_op jit(solution)/shard_map/kept/pallas_call | solution.py:199
  218.9 6.3 %all-to-all-done.6 = f32[16,1,384]{2,1,0:T(1,128)S(1)} async-done(((f32[16,1,384]{2,1,0:T(1,128)}), f32[16,1,384]{2,1,0:T(1,128)S(1)}, u32[]{:S(2)}, u32[]{:S(2)}) %all-to-all-start.6) | async-done | bytes 24608 | tf_op jit(solution)/shard_map/all_to_all | solution.py:224
  (50 shorter events, 27.8 us)
Async XLA Ops:
  0.6 28.2 %copy-start = (s32[3,16]{1,0:T(4,128)S(1)}, s32[3,16]{1,0:T(4,128)}, u32[]{:S(2)}) copy-start(s32[3,16]{1,0:T(4,128)} %param.3) | copy-start | bytes 580
  25.3 16.6 %all-to-all-start.1 = ((f32[8,160,128]{2,1,0:T(8,128)}), f32[8,160,128]{2,1,0:T(8,128)S(1)}, u32[]{:S(2)}, u32[]{:S(2)}) async-start(f32[8,160,128]{2,1,0:T(8,128)} %broadcast_in_dim.8), calls=%async_computation.1 | async-start | bytes 1310720 | tf_op jit(solution)/shard_map/all_to_all | solution.py:218
  41.9 0.8 copy-start.5
  42.7 23.0 %copy-start.3 = (f32[1024,512]{1,0:T(8,128)S(1)}, f32[1024,512]{1,0:T(8,128)}, u32[]{:S(2)}) copy-start(f32[1024,512]{1,0:T(8,128)} %pair_ref.3) | copy-start | bytes 6291460
  63.3 14.4 %collective-permute-start = (f32[1024,256]{1,0:T(8,128)}, f32[1024,256]{1,0:T(8,128)S(1)}, u32[]{:S(2)}, u32[]{:S(2)}) collective-permute-start(f32[1024,256]{1,0:T(8,128)} %get-tuple-element.16), channel_id=1, source_target_pairs={{0,8},{8,16},{16,24},{24,32},{32,40},{40,48},{48,56},{56,64},{64,7... | collective-permute-start | bytes 3145736 | tf_op jit(solution)/shard_map/ppermute | solution.py:210
  70.8 14.2 %copy-start.10 = (f32[256,256]{1,0:T(8,128)S(1)}, f32[256,256]{1,0:T(8,128)}, u32[]{:S(2)}) copy-start(f32[256,256]{1,0:T(8,128)} %get-tuple-element.18) | copy-start | bytes 786436
  77.8 1.0 copy-start.2
  81.6 11.0 %all-to-all-start.2 = ((f32[8,32,256]{2,1,0:T(8,128)}), f32[8,32,256]{2,1,0:T(8,128)S(1)}, u32[]{:S(2)}, u32[]{:S(2)}) async-start(f32[8,32,256]{2,1,0:T(8,128)} %bitcast.10), calls=%async_computation.2 | async-start | bytes 524288 | tf_op jit(solution)/shard_map/all_to_all | solution.py:216
  85.0 11.7 %collective-permute-start.1 = (f32[256,256]{1,0:T(8,128)S(1)}, f32[256,256]{1,0:T(8,128)S(1)}, u32[]{:S(2)}, u32[]{:S(2)}) collective-permute-start(f32[256,256]{1,0:T(8,128)S(1)} %copy-done.10), channel_id=1, source_target_pairs={{0,8},{8,16},{16,24},{24,32},{32,40},{40,48},{48,56},{56,64},{64,7... | collective-permute-start | bytes 786440 | tf_op jit(solution)/shard_map/ppermute | solution.py:210
  93.3 11.0 %all-to-all-start.3 = ((f32[8,32,256]{2,1,0:T(8,128)}), f32[8,32,256]{2,1,0:T(8,128)S(1)}, u32[]{:S(2)}, u32[]{:S(2)}) async-start(f32[8,32,256]{2,1,0:T(8,128)} %broadcast_in_dim.9), calls=%async_computation.3 | async-start | bytes 524288 | tf_op jit(solution)/shard_map/all_to_all | solution.py:218
  96.8 7.6 %copy-start.13 = (f32[256,256]{1,0:T(8,128)}, f32[256,256]{1,0:T(8,128)S(1)}, u32[]{:S(2)}) copy-start(f32[256,256]{1,0:T(8,128)S(1)} %collective-permute-done.1.right_diag_ref) | copy-start | bytes 786436
  104.3 0.7 copy-start.7
  137.3 16.8 %collective-permute-start.2 = (f32[1024,256]{1,0:T(8,128)}, f32[1024,256]{1,0:T(8,128)S(1)}, u32[]{:S(2)}, u32[]{:S(2)}) collective-permute-start(f32[1024,256]{1,0:T(8,128)} %get-tuple-element.20), channel_id=1, source_target_pairs={{0,8},{8,16},{16,24},{24,32},{32,40},{40,48},{48,56},{56,64},{64,7... | collective-permute-start | bytes 3145736 | tf_op jit(solution)/shard_map/ppermute | solution.py:210
  145.7 15.7 %copy-start.11 = (f32[256,256]{1,0:T(8,128)S(1)}, f32[256,256]{1,0:T(8,128)}, u32[]{:S(2)}) copy-start(f32[256,256]{1,0:T(8,128)} %get-tuple-element.22) | copy-start | bytes 786436
  154.1 1.0 copy-start.1
  158.0 11.0 %all-to-all-start.4 = ((f32[8,32,256]{2,1,0:T(8,128)}), f32[8,32,256]{2,1,0:T(8,128)S(1)}, u32[]{:S(2)}, u32[]{:S(2)}) async-start(f32[8,32,256]{2,1,0:T(8,128)} %bitcast.11), calls=%async_computation.4 | async-start | bytes 524288 | tf_op jit(solution)/shard_map/all_to_all | solution.py:216
  161.4 11.7 %collective-permute-start.3 = (f32[256,256]{1,0:T(8,128)S(1)}, f32[256,256]{1,0:T(8,128)S(1)}, u32[]{:S(2)}, u32[]{:S(2)}) collective-permute-start(f32[256,256]{1,0:T(8,128)S(1)} %copy-done.11), channel_id=1, source_target_pairs={{0,8},{8,16},{16,24},{24,32},{32,40},{40,48},{48,56},{56,64},{64,7... | collective-permute-start | bytes 786440 | tf_op jit(solution)/shard_map/ppermute | solution.py:210
  169.7 11.0 %all-to-all-start.5 = ((f32[8,32,256]{2,1,0:T(8,128)}), f32[8,32,256]{2,1,0:T(8,128)S(1)}, u32[]{:S(2)}, u32[]{:S(2)}) async-start(f32[8,32,256]{2,1,0:T(8,128)} %broadcast_in_dim.10), calls=%async_computation.5 | async-start | bytes 524288 | tf_op jit(solution)/shard_map/all_to_all | solution.py:218
  173.1 7.6 %copy-start.12 = (f32[256,256]{1,0:T(8,128)}, f32[256,256]{1,0:T(8,128)S(1)}, u32[]{:S(2)}) copy-start(f32[256,256]{1,0:T(8,128)S(1)} %collective-permute-done.3.right_diag_ref) | copy-start | bytes 786436
  181.4 24.8 %copy-start.8 = (f32[1,128]{1,0:T(1,128)S(1)}, f32[1,128]{1,0:T(1,128)}, u32[]{:S(2)}) copy-start(f32[1,128]{1,0:T(1,128)} %get-tuple-element.25) | copy-start | bytes 1540
  181.4 24.8 %copy-start.9 = (f32[1,128]{1,0:T(1,128)S(1)}, f32[1,128]{1,0:T(1,128)}, u32[]{:S(2)}) copy-start(f32[1,128]{1,0:T(1,128)} %get-tuple-element.26) | copy-start | bytes 1540
  201.5 24.4 %collective-permute-start.4 = (f32[1024,256]{1,0:T(8,128)}, f32[1024,256]{1,0:T(8,128)S(1)}, u32[]{:S(2)}, u32[]{:S(2)}) collective-permute-start(f32[1024,256]{1,0:T(8,128)} %get-tuple-element.24), channel_id=1, source_target_pairs={{0,8},{8,16},{16,24},{24,32},{32,40},{40,48},{48,56},{56,64},{64,7... | collective-permute-start | bytes 3145736 | tf_op jit(solution)/shard_map/ppermute | solution.py:210
  207.5 17.7 %all-to-all-start.6 = ((f32[16,1,384]{2,1,0:T(1,128)}), f32[16,1,384]{2,1,0:T(1,128)S(1)}, u32[]{:S(2)}, u32[]{:S(2)}) async-start(f32[16,1,384]{2,1,0:T(1,128)} %broadcast_in_dim.11), calls=%async_computation.6 | async-start | bytes 49152 | tf_op jit(solution)/shard_map/all_to_all | solution.py:224
  226.0 1.0 copy-start.4
  (1 other events, 0.7 us)
